TPU v7x, 32 devices: a whole 2x2x4 slice. The times are simulated.
32 devices in a mesh: dp: 8 (over z, y), mp: 4 (over x, core).
Axes of the slice: x: 2, y: 2, z: 4, core: 2. Of those that a mesh axis runs over, the one named last changes fastest.
Arguments:
- clean_latent: float32 [16, 768, 20], P('dp', 'mp'), may hold values from -6 to 6
- noise_draw: float32 [16, 768, 20], P('dp', 'mp'), may hold values from -6 to 6
- captions: bfloat16 [16, 256, 768], P('dp'), may hold values from -6 to 6
- caption_len: int32 [16], P('dp'), may hold values from 5 to 256, as said below
- timestep: int32 [16], P('dp'), may hold values from 0 to 999
- step_weight: float32 [1000], replicated, may hold values from 0.25 to 4
- step_count: int32 [1], replicated, may hold values from 2 to 20
- unit_slot: int32 [26], replicated, may hold values from 0 to 39, as said below
- master: float32 [40, 768, 768], P('dp', 'mp'), may hold values from -0.21875 to 0.21875
- first_moment: float32 [40, 768, 768], P('dp', 'mp'), may hold values from -8.34465e-07 to 8.34465e-07
- second_moment: float32 [40, 768, 768], P('dp', 'mp'), may hold values from 2.6031255e-16 to 1.0412502e-15
- latent_master: float32 [2, 20, 768], replicated, may hold values from -0.21875 to 0.21875
- latent_first: float32 [2, 20, 768], replicated, may hold values from -4.7683716e-06 to 4.7683716e-06
- latent_second: float32 [2, 20, 768], replicated, may hold values from 9.300595e-15 to 3.720238e-14
Outputs:
- updated_master: float32 [40, 768, 768], P('dp', 'mp')
- updated_first: float32 [40, 768, 768], P('dp', 'mp')
- updated_second: float32 [40, 768, 768], P('dp', 'mp')
- latent_updated: float32 [2, 20, 768], replicated
- latent_first_out: float32 [2, 20, 768], replicated
- latent_second_out: float32 [2, 20, 768], replicated
- grad_norm: float32 [], replicated
- loss_value: float32 [], replicated
Inputs may be any that keep to these rules, and one draw needn't show every extreme that they name: Clip b's caption occupies its first caption_len[b] token slots; some clip uses all 256. All entries differ, so every place holds at most one matrix; matrix u is owned by dp index unit_slot[u] // 5 in its place unit_slot[u] % 5; some dp index owns 5 matrices, every other index owns 0 to 5.
All inputs are finite; a program needn't handle non-finite values.
Results may differ from a plain program's by a relative error of at most 0.017.
Values may be sent and summed in bfloat16 or wider, within the bound.
No kernel may reach another device: no remote copies, remote signals or barrier semaphores. Data moves between devices by JAX's collectives and lax.ppermute only.
A program may use at most 192 MiB of HBM per device.

v0:
```python
import math
import jax
import jax.numpy as jnp
from jax import lax
from jax.sharding import PartitionSpec as P

D = 768
HD = 64
C = 20
FRAMES = 768
NT = 1000
UNITS = 26
highest = lax.Precision.HIGHEST
beta_first = 0.9
beta_second = 0.999
adam_epsilon = 1e-08
learn_rate = 0.02
decay_rate = 0.1
clip_limit = 0.002
norm_epsilon = 1e-06
masked_score = -1e30
bfloat = jnp.bfloat16
single = jnp.float32


def broadcast(array, axis, root):
    mine = lax.axis_index(axis) == root
    return lax.psum(jnp.where(mine, array, jnp.zeros_like(array)), axis)


def normed(values):
    center = values - jnp.mean(values, axis=-1, keepdims=True)
    spread_sq = jnp.mean(center * center, axis=-1, keepdims=True)
    return center * lax.rsqrt(spread_sq + norm_epsilon)


def modulate(values, shift, scale):
    return normed(values) * (1.0 + scale[:, None, :]) + shift[:, None, :]


def modulate_back(values, shift, scale, grad):
    _, pullback = jax.vjp(modulate, values, shift, scale)
    return pullback(grad)


def adamw(weight, moment, square, grad, count):
    moment = beta_first * moment + (1.0 - beta_first) * grad
    square = beta_second * square + (1.0 - beta_second) * grad * grad
    first_fix = 1.0 - jnp.power(beta_first, count)
    second_fix = 1.0 - jnp.power(beta_second, count)
    update = (
        moment / first_fix / (jnp.sqrt(square / second_fix) + adam_epsilon) + decay_rate * weight
    )
    return (weight - learn_rate * update, moment, square)


def sinusoid(timestep):
    half_width = D // 2
    frequency = jnp.exp(-math.log(10000.0) * jnp.arange(half_width).astype(single) / half_width)
    angles = timestep.astype(single)[:, None] * frequency[None, :]
    return jnp.concatenate([jnp.cos(angles), jnp.sin(angles)], axis=1)


def matmul(form, left, right):
    return jnp.einsum(form, left, right, preferred_element_type=single)


def masked_scores(query, keys, mask):
    scores = matmul("fhk,ghk->hfg", query, keys) * HD ** (-0.5)
    return jnp.where(mask[None, None, :], scores, masked_score)


def attend_forward(parts):
    query, keys, values, mask = parts
    scores = masked_scores(query, keys, mask)
    row_max = jnp.max(scores, axis=-1, keepdims=True)
    shifted = jnp.exp(scores - row_max)
    row_total = jnp.sum(shifted, axis=-1, keepdims=True)
    probs = shifted / row_total
    output = matmul("hfg,ghk->fhk", probs.astype(bfloat), values)
    return (output.astype(bfloat), (row_max + jnp.log(row_total))[..., 0])


def attend_backward(parts):
    query, keys, values, mask, grad_out, log_total = parts
    probs = jnp.exp(masked_scores(query, keys, mask) - log_total[..., None])
    grad_probs = matmul("fhk,ghk->hfg", grad_out, values)
    inner = jnp.sum(probs * grad_probs, axis=-1, keepdims=True)
    grad_scores = (probs * (grad_probs - inner)).astype(bfloat)
    grad_query = matmul("hfg,ghk->fhk", grad_scores, keys) * HD ** (-0.5)
    grad_keys = matmul("hfg,fhk->ghk", grad_scores, query) * HD ** (-0.5)
    grad_values = matmul("hfg,fhk->ghk", probs.astype(bfloat), grad_out)
    return (grad_query.astype(bfloat), grad_keys.astype(bfloat), grad_values.astype(bfloat))


def split_heads(values):
    return values.reshape(values.shape[0], values.shape[1], -1, HD)


def merge_heads(values):
    return values.reshape(values.shape[0], values.shape[1], -1)


def attention(query, keys, values, mask):
    output, log_total = lax.map(
        attend_forward, (split_heads(query), split_heads(keys), split_heads(values), mask)
    )
    return (merge_heads(output), log_total)


def attention_back(query, keys, values, mask, grad_out, log_total):
    grads = lax.map(
        attend_backward,
        (
            split_heads(query),
            split_heads(keys),
            split_heads(values),
            mask,
            split_heads(grad_out),
            log_total,
        ),
    )
    return tuple((merge_heads(item) for item in grads))


def spread(values):
    return lax.all_gather(values, "mp", axis=1, tiled=True)


def collect(values):
    return lax.psum_scatter(
        values.astype(jnp.bfloat16), "mp", scatter_dimension=1, tiled=True
    ).astype(jnp.float32)


def side_by_side(stack):
    return jnp.transpose(stack, (1, 0, 2)).reshape(stack.shape[1], -1)


def body(
    clean_latent,
    noise_draw,
    captions,
    caption_len,
    timestep,
    step_weight,
    step_count,
    unit_slot,
    master,
    first_moment,
    second_moment,
    latent_master,
    latent_first,
    latent_second,
):
    slots = master.shape[0]
    owner = unit_slot // slots
    place = unit_slot % slots

    def fetch_one(running, index):
        local = lax.dynamic_index_in_dim(master, place[index], 0, keepdims=False).astype(bfloat)
        return (running, broadcast(local, "dp", owner[index]))

    _, fetched = lax.scan(fetch_one, 0, jnp.arange(UNITS))
    weights = jnp.swapaxes(fetched, 1, 2)
    width = weights.shape[2]
    table = jnp.arange(step_weight.shape[0])
    clip_weight = jnp.sum(
        jnp.where(timestep[:, None] == table[None, :], step_weight[None, :], 0.0), axis=1
    )
    weight_total = lax.psum(jnp.sum(clip_weight), "dp")
    level = (timestep.astype(single) + 0.5) / NT
    noisy = (1.0 - level)[:, None, None] * clean_latent + level[:, None, None] * noise_draw
    target = noise_draw - clean_latent
    cap_mask = jnp.arange(captions.shape[1])[None, :] < caption_len[:, None]
    pooled = (
        jnp.sum(jnp.where(cap_mask[:, :, None], captions.astype(single), 0.0), axis=1)
        / caption_len.astype(single)[:, None]
    )
    sinus_low = sinusoid(timestep).astype(bfloat)
    pooled_low = pooled.astype(bfloat)
    cond_part = matmul("bd,de->be", sinus_low, weights[24]) + matmul(
        "bd,de->be", pooled_low, weights[25]
    )
    cond = lax.all_gather(cond_part, "mp", axis=1, tiled=True)
    active = jax.nn.silu(cond).astype(bfloat)
    modulation = lax.all_gather(
        matmul("bd,jde->bje", active, weights[16:24]), "mp", axis=2, tiled=True
    )
    hidden_zero = jnp.einsum("bfc,cd->bfd", noisy, latent_master[0], precision=highest)
    w_attn = side_by_side(weights[0:3])
    first_in = spread(modulate(hidden_zero, modulation[:, 0], modulation[:, 1]).astype(bfloat))
    self_proj = matmul("bfd,de->bfe", first_in, w_attn).astype(bfloat)
    self_query, self_keys, self_values = jnp.split(self_proj, 3, axis=2)
    self_mask = jnp.ones((self_query.shape[0], self_query.shape[1]), bool)
    self_flat, self_total = attention(self_query, self_keys, self_values, self_mask)
    self_branch = collect(matmul("bfk,dk->bfd", self_flat, weights[3]))
    hidden_one = hidden_zero + modulation[:, 2, None, :] * self_branch
    second_in = spread(normed(hidden_one).astype(bfloat))
    cross_query = matmul("bfd,de->bfe", second_in, weights[4]).astype(bfloat)
    w_text = side_by_side(weights[5:7])
    cross_keys, cross_values = jnp.split(
        matmul("bld,de->ble", captions, w_text).astype(bfloat), 2, axis=2
    )
    cross_flat, cross_total = attention(cross_query, cross_keys, cross_values, cap_mask)
    cross_branch = collect(matmul("bfk,dk->bfd", cross_flat, weights[7]))
    hidden_two = hidden_one + cross_branch
    w_up = side_by_side(weights[8:12])
    w_down = side_by_side(weights[12:16])
    third_in = spread(modulate(hidden_two, modulation[:, 3], modulation[:, 4]).astype(bfloat))
    upper_wide = matmul("bfd,dk->bfk", third_in, w_up).astype(bfloat).astype(single)
    activated = jax.nn.gelu(upper_wide, approximate=True).astype(bfloat)
    mlp_branch = collect(matmul("bfk,dk->bfd", activated, w_down))
    hidden_three = hidden_two + modulation[:, 5, None, :] * mlp_branch
    final_wide = (
        modulate(hidden_three, modulation[:, 6], modulation[:, 7]).astype(bfloat).astype(single)
    )
    predicted = jnp.einsum("bfd,cd->bfc", final_wide, latent_master[1], precision=highest)
    error = predicted - target
    loss_local = jnp.sum(clip_weight[:, None, None] * error * error)
    grad_pred = 2.0 / (C * FRAMES) * clip_weight[:, None, None] * error / weight_total
    grad_out_proj = jnp.einsum("bfc,bfd->cd", grad_pred, final_wide, precision=highest)
    grad_final = jnp.einsum("bfc,cd->bfd", grad_pred, latent_master[1], precision=highest)
    grad_three, shift_f, scale_f = modulate_back(
        hidden_three, modulation[:, 6], modulation[:, 7], grad_final
    )
    gate_m_grad = jnp.sum(grad_three * mlp_branch, axis=1)
    grad_mlp = spread((modulation[:, 5, None, :] * grad_three).astype(bfloat))
    grad_act = matmul("bfd,dk->bfk", grad_mlp, w_down)
    grad_w_down = matmul("bfd,bfk->dk", grad_mlp, activated)
    _, gelu_back = jax.vjp(lambda inner_in: jax.nn.gelu(inner_in, approximate=True), upper_wide)
    grad_upper = gelu_back(grad_act)[0].astype(bfloat)
    grad_w_up = matmul("bfd,bfk->dk", third_in, grad_upper)
    grad_third = collect(matmul("bfk,dk->bfd", grad_upper, w_up))
    grad_two, shift_m, scale_m = modulate_back(
        hidden_two, modulation[:, 3], modulation[:, 4], grad_third
    )
    grad_two = grad_two + grad_three
    grad_cross = spread(grad_two.astype(bfloat))
    grad_cross_flat = matmul("bfd,dk->bfk", grad_cross, weights[7]).astype(bfloat)
    grad_w_cross_out = matmul("bfd,bfk->dk", grad_cross, cross_flat)
    cq_grad, ck_grad, cv_grad = attention_back(
        cross_query, cross_keys, cross_values, cap_mask, grad_cross_flat, cross_total
    )
    grad_w_cq = matmul("bfd,bfk->dk", second_in, cq_grad)
    grad_w_text = matmul("bld,ble->de", captions, jnp.concatenate([ck_grad, cv_grad], axis=2))
    grad_second = collect(matmul("bfk,dk->bfd", cq_grad, weights[4]))
    _, norm_back = jax.vjp(normed, hidden_one)
    grad_one = grad_two + norm_back(grad_second)[0]
    gate_a_grad = jnp.sum(grad_one * self_branch, axis=1)
    grad_self = spread((modulation[:, 2, None, :] * grad_one).astype(bfloat))
    grad_self_flat = matmul("bfd,dk->bfk", grad_self, weights[3]).astype(bfloat)
    grad_w_self_out = matmul("bfd,bfk->dk", grad_self, self_flat)
    sq_grad, sk_grad, sv_grad = attention_back(
        self_query, self_keys, self_values, self_mask, grad_self_flat, self_total
    )
    grad_proj = jnp.concatenate([sq_grad, sk_grad, sv_grad], axis=2)
    grad_w_attn = matmul("bfd,bfe->de", first_in, grad_proj)
    grad_first = collect(matmul("bfe,de->bfd", grad_proj, w_attn))
    grad_zero, shift_a, scale_a = modulate_back(
        hidden_zero, modulation[:, 0], modulation[:, 1], grad_first
    )
    grad_zero = grad_zero + grad_one
    grad_in_proj = jnp.einsum("bfc,bfd->cd", noisy, grad_zero, precision=highest)
    grad_mod = jnp.stack(
        [shift_a, scale_a, gate_a_grad, shift_m, scale_m, gate_m_grad, shift_f, scale_f], axis=1
    )
    mod_own = (
        lax.psum_scatter(grad_mod.astype(jnp.bfloat16), "mp", scatter_dimension=2, tiled=True)
        .astype(jnp.float32)
        .astype(bfloat)
    )
    grad_ada = matmul("bd,bje->jde", active, mod_own)
    grad_active = matmul("bje,jde->bd", mod_own, weights[16:24])
    _, silu_back = jax.vjp(jax.nn.silu, cond)
    cond_own = lax.psum_scatter(
        silu_back(grad_active)[0], "mp", scatter_dimension=1, tiled=True
    ).astype(bfloat)
    grad_time = matmul("bd,be->de", sinus_low, cond_own)
    grad_pool = matmul("bd,be->de", pooled_low, cond_own)

    def columns(matrix, count):
        return jnp.transpose(matrix.reshape(matrix.shape[0], count, width), (1, 0, 2))

    grads_cols = jnp.concatenate(
        [
            columns(grad_w_attn, 3),
            grad_w_self_out[None],
            grad_w_cq[None],
            columns(grad_w_text, 2),
            grad_w_cross_out[None],
            columns(grad_w_up, 4),
            columns(grad_w_down, 4),
            grad_ada,
            grad_time[None],
            grad_pool[None],
        ],
        axis=0,
    )
    grads = jnp.swapaxes(grads_cols, 1, 2)
    local_ids = lax.axis_index("dp") * slots + jnp.arange(slots)
    pick = (unit_slot[None, :] == local_ids[:, None]).astype(single)
    live_slot = jnp.sum(pick, axis=1) > 0.5
    summed = lax.psum(grads, "dp")
    owned = jnp.einsum("su,ude->sde", pick, summed, precision=highest)
    latent_grad, loss_sum = lax.psum(
        (jnp.stack([grad_in_proj, grad_out_proj]), loss_local), ("dp", "mp")
    )
    square_sum = lax.psum(jnp.sum(owned * owned), ("dp", "mp")) + jnp.sum(latent_grad * latent_grad)
    grad_norm = jnp.sqrt(square_sum)
    factor = clip_limit / jnp.maximum(grad_norm, clip_limit)
    count = step_count[0].astype(single)
    new_weight, new_moment, new_square = adamw(
        master, first_moment, second_moment, owned * factor, count
    )
    keep = live_slot[:, None, None]
    latent_weight, latent_moment, latent_square = adamw(
        latent_master, latent_first, latent_second, latent_grad * factor, count
    )
    loss_value = loss_sum / (C * FRAMES * weight_total)
    return (
        jnp.where(keep, new_weight, master),
        jnp.where(keep, new_moment, first_moment),
        jnp.where(keep, new_square, second_moment),
        latent_weight,
        latent_moment,
        latent_square,
        grad_norm,
        loss_value,
    )


def solution(mesh):
    placed = (
        P("dp", "mp", None),
        P("dp", "mp", None),
        P("dp", None, None),
        P("dp"),
        P("dp"),
        P(),
        P(),
        P(),
        P("dp", "mp", None),
        P("dp", "mp", None),
        P("dp", "mp", None),
        P(),
        P(),
        P(),
    )
    return jax.shard_map(
        body,
        mesh=mesh,
        in_specs=placed,
        out_specs=(
            P("dp", "mp", None),
            P("dp", "mp", None),
            P("dp", "mp", None),
            P(),
            P(),
            P(),
            P(),
            P(),
        ),
        check_vma=False,
    )
```

profile of v0, /device:TPU:0, one launch (start us, length us, event | category | flops | bytes accessed | tf_op | source)
XLA Modules:
  0.0 3431.0 jit_solution(15511548824490936030)
XLA Ops:
  17.4 2054.4 %while.62 = (s32[]{:T(128)}, bf16[26,192,768]{2,1,0:T(8,128)(2,1)}, s32[26]{0:T(128)S(1)}, s32[26]{0:T(128)S(1)}, s32[26]{0:T(128)S(1)}, /*index=5*/bf16[5,192,7...) while((s32[]{:T(128)}, bf16[26,192,768]{2,1,0:T(8,128)(2,1)}, ...), condition=%wide.region_5.6_spmd, body=%wide.region_3.5_spmd.sunk | while | flops 294924 | bytes 2949439 | solution.py:164
  24.6 73.7 %all-reduce.9.cloned.1.call-done = bf16[1,192,768]{2,1,0:T(8,128)(2,1)} async-done(((bf16[1,192,768]{2,1,0:T(8,128)(2,1)}), bf16[1,192,768]{2,1,0:T(8,128)(2,1)}) %all-reduce.9.cloned.1.call-update) | async-done | bytes 294928 | tf_op jit(solution)/shard_map/while/body/eval_jaxpr/psum | solution.py:28
  107.0 70.1 %all-reduce.9.cloned.1.call-done = bf16[1,192,768]{2,1,0:T(8,128)(2,1)} async-done(((bf16[1,192,768]{2,1,0:T(8,128)(2,1)}), bf16[1,192,768]{2,1,0:T(8,128)(2,1)}) %all-reduce.9.cloned.1.call-update) | async-done | bytes 294928 | tf_op jit(solution)/shard_map/while/body/eval_jaxpr/psum | solution.py:28
  185.9 70.1 %all-reduce.9.cloned.1.call-done = bf16[1,192,768]{2,1,0:T(8,128)(2,1)} async-done(((bf16[1,192,768]{2,1,0:T(8,128)(2,1)}), bf16[1,192,768]{2,1,0:T(8,128)(2,1)}) %all-reduce.9.cloned.1.call-update) | async-done | bytes 294928 | tf_op jit(solution)/shard_map/while/body/eval_jaxpr/psum | solution.py:28
  264.7 70.1 %all-reduce.9.cloned.1.call-done = bf16[1,192,768]{2,1,0:T(8,128)(2,1)} async-done(((bf16[1,192,768]{2,1,0:T(8,128)(2,1)}), bf16[1,192,768]{2,1,0:T(8,128)(2,1)}) %all-reduce.9.cloned.1.call-update) | async-done | bytes 294928 | tf_op jit(solution)/shard_map/while/body/eval_jaxpr/psum | solution.py:28
  343.6 70.1 %all-reduce.9.cloned.1.call-done = bf16[1,192,768]{2,1,0:T(8,128)(2,1)} async-done(((bf16[1,192,768]{2,1,0:T(8,128)(2,1)}), bf16[1,192,768]{2,1,0:T(8,128)(2,1)}) %all-reduce.9.cloned.1.call-update) | async-done | bytes 294928 | tf_op jit(solution)/shard_map/while/body/eval_jaxpr/psum | solution.py:28
  422.5 70.1 %all-reduce.9.cloned.1.call-done = bf16[1,192,768]{2,1,0:T(8,128)(2,1)} async-done(((bf16[1,192,768]{2,1,0:T(8,128)(2,1)}), bf16[1,192,768]{2,1,0:T(8,128)(2,1)}) %all-reduce.9.cloned.1.call-update) | async-done | bytes 294928 | tf_op jit(solution)/shard_map/while/body/eval_jaxpr/psum | solution.py:28
  501.3 70.1 %all-reduce.9.cloned.1.call-done = bf16[1,192,768]{2,1,0:T(8,128)(2,1)} async-done(((bf16[1,192,768]{2,1,0:T(8,128)(2,1)}), bf16[1,192,768]{2,1,0:T(8,128)(2,1)}) %all-reduce.9.cloned.1.call-update) | async-done | bytes 294928 | tf_op jit(solution)/shard_map/while/body/eval_jaxpr/psum | solution.py:28
  580.2 70.1 %all-reduce.9.cloned.1.call-done = bf16[1,192,768]{2,1,0:T(8,128)(2,1)} async-done(((bf16[1,192,768]{2,1,0:T(8,128)(2,1)}), bf16[1,192,768]{2,1,0:T(8,128)(2,1)}) %all-reduce.9.cloned.1.call-update) | async-done | bytes 294928 | tf_op jit(solution)/shard_map/while/body/eval_jaxpr/psum | solution.py:28
  659.1 70.1 %all-reduce.9.cloned.1.call-done = bf16[1,192,768]{2,1,0:T(8,128)(2,1)} async-done(((bf16[1,192,768]{2,1,0:T(8,128)(2,1)}), bf16[1,192,768]{2,1,0:T(8,128)(2,1)}) %all-reduce.9.cloned.1.call-update) | async-done | bytes 294928 | tf_op jit(solution)/shard_map/while/body/eval_jaxpr/psum | solution.py:28
  738.0 70.1 %all-reduce.9.cloned.1.call-done = bf16[1,192,768]{2,1,0:T(8,128)(2,1)} async-done(((bf16[1,192,768]{2,1,0:T(8,128)(2,1)}), bf16[1,192,768]{2,1,0:T(8,128)(2,1)}) %all-reduce.9.cloned.1.call-update) | async-done | bytes 294928 | tf_op jit(solution)/shard_map/while/body/eval_jaxpr/psum | solution.py:28
  816.9 70.1 %all-reduce.9.cloned.1.call-done = bf16[1,192,768]{2,1,0:T(8,128)(2,1)} async-done(((bf16[1,192,768]{2,1,0:T(8,128)(2,1)}), bf16[1,192,768]{2,1,0:T(8,128)(2,1)}) %all-reduce.9.cloned.1.call-update) | async-done | bytes 294928 | tf_op jit(solution)/shard_map/while/body/eval_jaxpr/psum | solution.py:28
  895.7 70.1 %all-reduce.9.cloned.1.call-done = bf16[1,192,768]{2,1,0:T(8,128)(2,1)} async-done(((bf16[1,192,768]{2,1,0:T(8,128)(2,1)}), bf16[1,192,768]{2,1,0:T(8,128)(2,1)}) %all-reduce.9.cloned.1.call-update) | async-done | bytes 294928 | tf_op jit(solution)/shard_map/while/body/eval_jaxpr/psum | solution.py:28
  974.6 70.1 %all-reduce.9.cloned.1.call-done = bf16[1,192,768]{2,1,0:T(8,128)(2,1)} async-done(((bf16[1,192,768]{2,1,0:T(8,128)(2,1)}), bf16[1,192,768]{2,1,0:T(8,128)(2,1)}) %all-reduce.9.cloned.1.call-update) | async-done | bytes 294928 | tf_op jit(solution)/shard_map/while/body/eval_jaxpr/psum | solution.py:28
  1053.4 70.1 %all-reduce.9.cloned.1.call-done = bf16[1,192,768]{2,1,0:T(8,128)(2,1)} async-done(((bf16[1,192,768]{2,1,0:T(8,128)(2,1)}), bf16[1,192,768]{2,1,0:T(8,128)(2,1)}) %all-reduce.9.cloned.1.call-update) | async-done | bytes 294928 | tf_op jit(solution)/shard_map/while/body/eval_jaxpr/psum | solution.py:28
  1132.3 70.1 %all-reduce.9.cloned.1.call-done = bf16[1,192,768]{2,1,0:T(8,128)(2,1)} async-done(((bf16[1,192,768]{2,1,0:T(8,128)(2,1)}), bf16[1,192,768]{2,1,0:T(8,128)(2,1)}) %all-reduce.9.cloned.1.call-update) | async-done | bytes 294928 | tf_op jit(solution)/shard_map/while/body/eval_jaxpr/psum | solution.py:28
  1211.2 70.1 %all-reduce.9.cloned.1.call-done = bf16[1,192,768]{2,1,0:T(8,128)(2,1)} async-done(((bf16[1,192,768]{2,1,0:T(8,128)(2,1)}), bf16[1,192,768]{2,1,0:T(8,128)(2,1)}) %all-reduce.9.cloned.1.call-update) | async-done | bytes 294928 | tf_op jit(solution)/shard_map/while/body/eval_jaxpr/psum | solution.py:28
  1290.1 70.1 %all-reduce.9.cloned.1.call-done = bf16[1,192,768]{2,1,0:T(8,128)(2,1)} async-done(((bf16[1,192,768]{2,1,0:T(8,128)(2,1)}), bf16[1,192,768]{2,1,0:T(8,128)(2,1)}) %all-reduce.9.cloned.1.call-update) | async-done | bytes 294928 | tf_op jit(solution)/shard_map/while/body/eval_jaxpr/psum | solution.py:28
  1369.0 70.1 %all-reduce.9.cloned.1.call-done = bf16[1,192,768]{2,1,0:T(8,128)(2,1)} async-done(((bf16[1,192,768]{2,1,0:T(8,128)(2,1)}), bf16[1,192,768]{2,1,0:T(8,128)(2,1)}) %all-reduce.9.cloned.1.call-update) | async-done | bytes 294928 | tf_op jit(solution)/shard_map/while/body/eval_jaxpr/psum | solution.py:28
  1447.9 70.1 %all-reduce.9.cloned.1.call-done = bf16[1,192,768]{2,1,0:T(8,128)(2,1)} async-done(((bf16[1,192,768]{2,1,0:T(8,128)(2,1)}), bf16[1,192,768]{2,1,0:T(8,128)(2,1)}) %all-reduce.9.cloned.1.call-update) | async-done | bytes 294928 | tf_op jit(solution)/shard_map/while/body/eval_jaxpr/psum | solution.py:28
  1526.7 70.1 %all-reduce.9.cloned.1.call-done = bf16[1,192,768]{2,1,0:T(8,128)(2,1)} async-done(((bf16[1,192,768]{2,1,0:T(8,128)(2,1)}), bf16[1,192,768]{2,1,0:T(8,128)(2,1)}) %all-reduce.9.cloned.1.call-update) | async-done | bytes 294928 | tf_op jit(solution)/shard_map/while/body/eval_jaxpr/psum | solution.py:28
  1605.6 70.1 %all-reduce.9.cloned.1.call-done = bf16[1,192,768]{2,1,0:T(8,128)(2,1)} async-done(((bf16[1,192,768]{2,1,0:T(8,128)(2,1)}), bf16[1,192,768]{2,1,0:T(8,128)(2,1)}) %all-reduce.9.cloned.1.call-update) | async-done | bytes 294928 | tf_op jit(solution)/shard_map/while/body/eval_jaxpr/psum | solution.py:28
  1684.5 70.1 %all-reduce.9.cloned.1.call-done = bf16[1,192,768]{2,1,0:T(8,128)(2,1)} async-done(((bf16[1,192,768]{2,1,0:T(8,128)(2,1)}), bf16[1,192,768]{2,1,0:T(8,128)(2,1)}) %all-reduce.9.cloned.1.call-update) | async-done | bytes 294928 | tf_op jit(solution)/shard_map/while/body/eval_jaxpr/psum | solution.py:28
  1763.4 70.1 %all-reduce.9.cloned.1.call-done = bf16[1,192,768]{2,1,0:T(8,128)(2,1)} async-done(((bf16[1,192,768]{2,1,0:T(8,128)(2,1)}), bf16[1,192,768]{2,1,0:T(8,128)(2,1)}) %all-reduce.9.cloned.1.call-update) | async-done | bytes 294928 | tf_op jit(solution)/shard_map/while/body/eval_jaxpr/psum | solution.py:28
  1842.2 70.1 %all-reduce.9.cloned.1.call-done = bf16[1,192,768]{2,1,0:T(8,128)(2,1)} async-done(((bf16[1,192,768]{2,1,0:T(8,128)(2,1)}), bf16[1,192,768]{2,1,0:T(8,128)(2,1)}) %all-reduce.9.cloned.1.call-update) | async-done | bytes 294928 | tf_op jit(solution)/shard_map/while/body/eval_jaxpr/psum | solution.py:28
  1921.1 70.1 %all-reduce.9.cloned.1.call-done = bf16[1,192,768]{2,1,0:T(8,128)(2,1)} async-done(((bf16[1,192,768]{2,1,0:T(8,128)(2,1)}), bf16[1,192,768]{2,1,0:T(8,128)(2,1)}) %all-reduce.9.cloned.1.call-update) | async-done | bytes 294928 | tf_op jit(solution)/shard_map/while/body/eval_jaxpr/psum | solution.py:28
  2000.0 70.1 %all-reduce.9.cloned.1.call-done = bf16[1,192,768]{2,1,0:T(8,128)(2,1)} async-done(((bf16[1,192,768]{2,1,0:T(8,128)(2,1)}), bf16[1,192,768]{2,1,0:T(8,128)(2,1)}) %all-reduce.9.cloned.1.call-update) | async-done | bytes 294928 | tf_op jit(solution)/shard_map/while/body/eval_jaxpr/psum | solution.py:28
  2101.1 21.8 all-gather.8.cloned.1.call-done
  2141.8 31.5 reduce-scatter.13.cloned.1.call-done
  2177.7 22.3 all-gather.10.cloned.1.call-done
  2216.1 29.8 reduce-scatter.15.cloned.1.call-done
  2253.0 20.8 all-gather.12.cloned.1.call-done
  2285.3 22.4 psum.42
  2326.2 24.0 all-gather.14.cloned.1.call-done
  2362.3 33.0 reduce-scatter.19.cloned.1.call-done
  2402.9 23.8 all-gather.16.cloned.1.call-done
  2431.0 14.6 while.65
  2449.1 33.0 reduce-scatter.21.cloned.1.call-done
  2490.4 24.0 all-gather.18.cloned.1.call-done
  2519.5 30.1 while.66
  2597.3 18.7 reduce-scatter.25.cloned.1.call-done
  2623.9 17.1 reduce-scatter.27.cloned.1.call-done
  2646.2 46.0 %concatenate.16 = f32[26,768,192]{1,0,2:T(8,128)} concatenate(f32[3,768,192]{1,0,2:T(4,128)S(1)} %bitcast.450, f32[1,768,192]{1,0,2:T(1,128)} %copy.315, f32[1,768,192]{1,0,2:T(1,128)} %copy.316, f32[2,768,192]{1,0,2:T(2,128)S(1)} %bitcast.466, f32[1,768,192]{1,0,2:T(1,128)} %copy.317, f32[4,768,192]{1,0,2:T(4,128)} %get-tuple-element.415, f32[4,768,192]{1,0,2:T(4,128)} %get-tuple-element.414, ...), dimensions={0} | concatenate | bytes 30670848 | tf_op jit(solution)/shard_map/concatenate | solution.py:285
  2693.8 73.2 %all-reduce.7.cloned.1.call-done = f32[2,20,768]{2,1,0:T(8,128)} async-done(((f32[2,20,768]{2,1,0:T(8,128)}), f32[2,20,768]{2,1,0:T(8,128)}) %all-reduce.7.cloned.1.call-update) | async-done | bytes 122896 | tf_op jit(solution)/shard_map/psum | solution.py:306
  2768.6 571.5 %all-reduce.5.cloned.1.call-done = f32[26,192,768]{2,0,1:T(8,128)} async-done(((f32[26,192,768]{2,0,1:T(8,128)}), f32[26,192,768]{2,0,1:T(8,128)}) %all-reduce.5.cloned.1.call-update) | async-done | bytes 15335440 | tf_op jit(solution)/shard_map/psum | solution.py:304
  3340.1 12.6 multiply_reduce_fusion.3
  3352.7 39.8 %all-reduce = (f32[]{:T(128)}, f32[]{:T(128)}) all-reduce(f32[]{:T(128)} %get-tuple-element.410, f32[]{:T(128)} %get-tuple-element.412), channel_id=1, replica_groups=mesh['dp'=8,'mp'=4] {'dp','mp'}, use_global_device_ids=true, to_apply=%region_54.55 | all-reduce | flops 2 | bytes 16 | tf_op jit(solution)/shard_map/psum | solution.py:309
  3397.2 15.7 copy_select_fusion
  (691 shorter events, 397.0 us)
Async XLA Ops:
  8.7 2064.3 %copy-start.110 = (f32[2]{0:T(128)}, f32[2]{0:T(128)S(1)}, u32[]{:S(2)}) copy-start(f32[2]{0:T(128)S(1)} %convert_element_type.199) | copy-start | bytes 28
  14.5 2158.8 %copy-start = (f32[2,192,768]{2,1,0:T(8,128)}, f32[2,192,768]{2,1,0:T(8,128)S(1)}, u32[]{:S(2)}) copy-start(f32[2,192,768]{2,1,0:T(8,128)S(1)} %get-tuple-element.408) | copy-start | bytes 3538948
  14.5 2084.2 %copy-start.75 = (f32[2,192]{1,0:T(2,128)}, f32[2,192]{1,0:T(2,128)S(1)}, u32[]{:S(2)}) copy-start(f32[2,192]{1,0:T(2,128)S(1)} %broadcast_multiply_fusion.3) | copy-start | bytes 4612
  14.9 2083.8 %copy-start.88 = (f32[2,192]{1,0:T(2,128)}, f32[2,192]{1,0:T(2,128)S(1)}, u32[]{:S(2)}) copy-start(f32[2,192]{1,0:T(2,128)S(1)} %fusion.188) | copy-start | bytes 4612
  17.1 2054.7 %copy-start.106 = (bf16[2,384]{1,0:T(2,128)(2,1)}, bf16[2,384]{1,0:T(2,128)(2,1)S(1)}, u32[]{:S(2)}) copy-start(bf16[2,384]{1,0:T(2,128)(2,1)S(1)} %get-tuple-element.401) | copy-start | bytes 4612
  17.4 2055.5 %copy-start.92 = (f32[2,768]{1,0:T(2,128)}, f32[2,768]{1,0:T(2,128)S(1)}, u32[]{:S(2)}) copy-start(f32[2,768]{1,0:T(2,128)S(1)} %select_reduce_fusion) | copy-start | bytes 18436
  17.4 80.8 %all-reduce.9.cloned.1.call-start = ((), (), s32[]{:S(2)}) async-start(), calls=%async_computation.24 | async-start | bytes 589824 | tf_op jit(solution)/shard_map/while/body/eval_jaxpr/psum | solution.py:28
  99.9 77.2 %all-reduce.9.cloned.1.call-start = ((), (), s32[]{:S(2)}) async-start(), calls=%async_computation.24 | async-start | bytes 589824 | tf_op jit(solution)/shard_map/while/body/eval_jaxpr/psum | solution.py:28
  178.8 77.2 %all-reduce.9.cloned.1.call-start = ((), (), s32[]{:S(2)}) async-start(), calls=%async_computation.24 | async-start | bytes 589824 | tf_op jit(solution)/shard_map/while/body/eval_jaxpr/psum | solution.py:28
  257.7 77.2 %all-reduce.9.cloned.1.call-start = ((), (), s32[]{:S(2)}) async-start(), calls=%async_computation.24 | async-start | bytes 589824 | tf_op jit(solution)/shard_map/while/body/eval_jaxpr/psum | solution.py:28
  336.5 77.2 %all-reduce.9.cloned.1.call-start = ((), (), s32[]{:S(2)}) async-start(), calls=%async_computation.24 | async-start | bytes 589824 | tf_op jit(solution)/shard_map/while/body/eval_jaxpr/psum | solution.py:28
  415.4 77.2 %all-reduce.9.cloned.1.call-start = ((), (), s32[]{:S(2)}) async-start(), calls=%async_computation.24 | async-start | bytes 589824 | tf_op jit(solution)/shard_map/while/body/eval_jaxpr/psum | solution.py:28
  494.3 77.2 %all-reduce.9.cloned.1.call-start = ((), (), s32[]{:S(2)}) async-start(), calls=%async_computation.24 | async-start | bytes 589824 | tf_op jit(solution)/shard_map/while/body/eval_jaxpr/psum | solution.py:28
  573.2 77.2 %all-reduce.9.cloned.1.call-start = ((), (), s32[]{:S(2)}) async-start(), calls=%async_computation.24 | async-start | bytes 589824 | tf_op jit(solution)/shard_map/while/body/eval_jaxpr/psum | solution.py:28
  652.0 77.2 %all-reduce.9.cloned.1.call-start = ((), (), s32[]{:S(2)}) async-start(), calls=%async_computation.24 | async-start | bytes 589824 | tf_op jit(solution)/shard_map/while/body/eval_jaxpr/psum | solution.py:28
  730.9 77.2 %all-reduce.9.cloned.1.call-start = ((), (), s32[]{:S(2)}) async-start(), calls=%async_computation.24 | async-start | bytes 589824 | tf_op jit(solution)/shard_map/while/body/eval_jaxpr/psum | solution.py:28
  809.8 77.2 %all-reduce.9.cloned.1.call-start = ((), (), s32[]{:S(2)}) async-start(), calls=%async_computation.24 | async-start | bytes 589824 | tf_op jit(solution)/shard_map/while/body/eval_jaxpr/psum | solution.py:28
  888.7 77.2 %all-reduce.9.cloned.1.call-start = ((), (), s32[]{:S(2)}) async-start(), calls=%async_computation.24 | async-start | bytes 589824 | tf_op jit(solution)/shard_map/while/body/eval_jaxpr/psum | solution.py:28
  967.5 77.2 %all-reduce.9.cloned.1.call-start = ((), (), s32[]{:S(2)}) async-start(), calls=%async_computation.24 | async-start | bytes 589824 | tf_op jit(solution)/shard_map/while/body/eval_jaxpr/psum | solution.py:28
  1046.4 77.2 %all-reduce.9.cloned.1.call-start = ((), (), s32[]{:S(2)}) async-start(), calls=%async_computation.24 | async-start | bytes 589824 | tf_op jit(solution)/shard_map/while/body/eval_jaxpr/psum | solution.py:28
  1125.3 77.2 %all-reduce.9.cloned.1.call-start = ((), (), s32[]{:S(2)}) async-start(), calls=%async_computation.24 | async-start | bytes 589824 | tf_op jit(solution)/shard_map/while/body/eval_jaxpr/psum | solution.py:28
  1204.1 77.2 %all-reduce.9.cloned.1.call-start = ((), (), s32[]{:S(2)}) async-start(), calls=%async_computation.24 | async-start | bytes 589824 | tf_op jit(solution)/shard_map/while/body/eval_jaxpr/psum | solution.py:28
  1283.0 77.2 %all-reduce.9.cloned.1.call-start = ((), (), s32[]{:S(2)}) async-start(), calls=%async_computation.24 | async-start | bytes 589824 | tf_op jit(solution)/shard_map/while/body/eval_jaxpr/psum | solution.py:28
  1361.9 77.2 %all-reduce.9.cloned.1.call-start = ((), (), s32[]{:S(2)}) async-start(), calls=%async_computation.24 | async-start | bytes 589824 | tf_op jit(solution)/shard_map/while/body/eval_jaxpr/psum | solution.py:28
  1440.8 77.2 %all-reduce.9.cloned.1.call-start = ((), (), s32[]{:S(2)}) async-start(), calls=%async_computation.24 | async-start | bytes 589824 | tf_op jit(solution)/shard_map/while/body/eval_jaxpr/psum | solution.py:28
  1519.7 77.2 %all-reduce.9.cloned.1.call-start = ((), (), s32[]{:S(2)}) async-start(), calls=%async_computation.24 | async-start | bytes 589824 | tf_op jit(solution)/shard_map/while/body/eval_jaxpr/psum | solution.py:28
  1598.5 77.2 %all-reduce.9.cloned.1.call-start = ((), (), s32[]{:S(2)}) async-start(), calls=%async_computation.24 | async-start | bytes 589824 | tf_op jit(solution)/shard_map/while/body/eval_jaxpr/psum | solution.py:28
  1677.4 77.2 %all-reduce.9.cloned.1.call-start = ((), (), s32[]{:S(2)}) async-start(), calls=%async_computation.24 | async-start | bytes 589824 | tf_op jit(solution)/shard_map/while/body/eval_jaxpr/psum | solution.py:28
  1756.3 77.2 %all-reduce.9.cloned.1.call-start = ((), (), s32[]{:S(2)}) async-start(), calls=%async_computation.24 | async-start | bytes 589824 | tf_op jit(solution)/shard_map/while/body/eval_jaxpr/psum | solution.py:28
  1835.2 77.2 %all-reduce.9.cloned.1.call-start = ((), (), s32[]{:S(2)}) async-start(), calls=%async_computation.24 | async-start | bytes 589824 | tf_op jit(solution)/shard_map/while/body/eval_jaxpr/psum | solution.py:28
  1914.0 77.2 %all-reduce.9.cloned.1.call-start = ((), (), s32[]{:S(2)}) async-start(), calls=%async_computation.24 | async-start | bytes 589824 | tf_op jit(solution)/shard_map/while/body/eval_jaxpr/psum | solution.py:28
  1992.9 77.2 %all-reduce.9.cloned.1.call-start = ((), (), s32[]{:S(2)}) async-start(), calls=%async_computation.24 | async-start | bytes 589824 | tf_op jit(solution)/shard_map/while/body/eval_jaxpr/psum | solution.py:28
  2071.8 51.1 %all-gather.8.cloned.1.call-start = ((), (), s32[]{:S(2)}) async-start(), calls=%async_computation.8 | async-start | bytes 2949120 | tf_op jit(solution)/shard_map/all_gather | solution.py:127
  2099.8 73.5 %reduce-scatter.13.cloned.1.call-start = ((), (), s32[]{:S(2)}) async-start(), calls=%async_computation.9 | async-start | bytes 2949120 | tf_op jit(solution)/shard_map/reduce_scatter | solution.py:131
  2140.2 59.7 %all-gather.10.cloned.1.call-start = ((), (), s32[]{:S(2)}) async-start(), calls=%async_computation.10 | async-start | bytes 2949120 | tf_op jit(solution)/shard_map/all_gather | solution.py:127
  2176.0 69.9 %reduce-scatter.15.cloned.1.call-start = ((), (), s32[]{:S(2)}) async-start(), calls=%async_computation.11 | async-start | bytes 2949120 | tf_op jit(solution)/shard_map/reduce_scatter | solution.py:131
  2212.9 60.9 %all-gather.12.cloned.1.call-start = ((), (), s32[]{:S(2)}) async-start(), calls=%async_computation.12 | async-start | bytes 2949120 | tf_op jit(solution)/shard_map/all_gather | solution.py:127
  2249.8 67.2 %reduce-scatter.17.cloned.1.call-start = ((), (), s32[]{:S(2)}) async-start(), calls=%async_computation.13 | async-start | bytes 2949120 | tf_op jit(solution)/shard_map/reduce_scatter | solution.py:131
  2283.8 66.3 %all-gather.14.cloned.1.call-start = ((), (), s32[]{:S(2)}) async-start(), calls=%async_computation.14 | async-start | bytes 2949120 | tf_op jit(solution)/shard_map/all_gather | solution.py:127
  2326.1 69.2 %reduce-scatter.19.cloned.1.call-start = ((), (), s32[]{:S(2)}) async-start(), calls=%async_computation.15 | async-start | bytes 2949120 | tf_op jit(solution)/shard_map/reduce_scatter | solution.py:131
  2362.3 64.5 %all-gather.16.cloned.1.call-start = ((), (), s32[]{:S(2)}) async-start(), calls=%async_computation.16 | async-start | bytes 2949120 | tf_op jit(solution)/shard_map/all_gather | solution.py:127
  2402.7 79.4 %reduce-scatter.21.cloned.1.call-start = ((), (), s32[]{:S(2)}) async-start(), calls=%async_computation.17 | async-start | bytes 2949120 | tf_op jit(solution)/shard_map/reduce_scatter | solution.py:131
  2449.0 65.3 %all-gather.18.cloned.1.call-start = ((), (), s32[]{:S(2)}) async-start(), calls=%async_computation.18 | async-start | bytes 2949120 | tf_op jit(solution)/shard_map/all_gather | solution.py:127
  2490.3 97.4 %reduce-scatter.23.cloned.1.call-start = ((), (), s32[]{:S(2)}) async-start(), calls=%async_computation.19 | async-start | bytes 2949120 | tf_op jit(solution)/shard_map/reduce_scatter | solution.py:131
  2554.6 61.4 %reduce-scatter.25.cloned.1.call-start = ((), (), s32[]{:S(2)}) async-start(), calls=%async_computation.22 | async-start | bytes 245760
  2596.1 44.9 %reduce-scatter.27.cloned.1.call-start = ((), (), s32[]{:S(2)}) async-start(), calls=%async_computation.23 | async-start | bytes 491520
  2620.2 146.9 %all-reduce.7.cloned.1.call-start = ((), (), s32[]{:S(2)}) async-start(), calls=%async_computation.21 | async-start | bytes 294912 | tf_op jit(solution)/shard_map/psum | solution.py:306
  2620.9 719.2 %all-reduce.5.cloned.1.call-start = ((), (), s32[]{:S(2)}) async-start(), calls=%async_computation.20 | async-start | bytes 37748736 | tf_op jit(solution)/shard_map/psum | solution.py:304
  (131 other events, 3364.9 us)
Sparse Core Ops, SparseCore 0:
  24.7 73.5 all-reduce.8
  107.1 69.9 all-reduce.8
  186.0 69.9 all-reduce.8
  264.8 69.9 all-reduce.8
  343.7 69.9 all-reduce.8
  422.6 69.9 all-reduce.8
  501.5 69.9 all-reduce.8
  580.3 69.9 all-reduce.8
  659.2 69.9 all-reduce.8
  738.1 69.9 all-reduce.8
  817.0 69.9 all-reduce.8
  895.8 69.9 all-reduce.8
  974.7 69.9 all-reduce.8
  1053.6 69.9 all-reduce.8
  1132.4 69.9 all-reduce.8
  1211.3 69.9 all-reduce.8
  1290.2 69.9 all-reduce.8
  1369.1 69.9 all-reduce.8
  1448.0 69.9 all-reduce.8
  1526.9 69.9 all-reduce.8
  1605.7 69.9 all-reduce.8
  1684.6 69.9 all-reduce.8
  1763.5 69.9 all-reduce.8
  1842.4 69.9 all-reduce.8
  1921.2 69.9 all-reduce.8
  2000.1 69.9 all-reduce.8
Sparse Core Ops, SparseCore 1:
  2099.9 23.0 all-gather.7
  2140.3 32.9 reduce-scatter.12
  2176.0 23.9 all-gather.9
  2212.9 32.9 reduce-scatter.14
  2249.8 23.9 all-gather.11
  2283.9 33.0 reduce-scatter.16
  2326.2 23.9 all-gather.13
  2362.3 32.9 reduce-scatter.18
  2402.8 23.9 all-gather.15
  2449.1 33.0 reduce-scatter.20
  2490.4 23.9 all-gather.17
  2554.7 33.0 reduce-scatter.22
  2596.2 19.7 reduce-scatter.24
  2620.2 20.7 reduce-scatter.26
  2646.6 120.4 all-reduce.6
  2771.1 568.9 all-reduce.4
where the time goes:
time: 3450 us; the launch traced here: 3430 us
  waiting for transfers between devices  2770 us (80%)
  local copies, waits for them, and re-layouts  219 us (6%)
  matrix products  128 us (4%)
  loops' own time  119 us (3%)
  other arithmetic  89.9 us (3%)
  blocking collectives  76.2 us (2%)
    psum x26, waiting for transfers between devices, broadcast(): return lax.psum(jnp.where(mine, array, jnp.zeros_like(array)), axis)  1830 us
    psum x1, waiting for transfers between devices, body(): summed = lax.psum(grads, 'dp')  571 us
    all_gather x6, waiting for transfers between devices, spread(): return lax.all_gather(values, 'mp', axis=1, tiled=True)  137 us
    reduce_scatter x6, waiting for transfers between devices, collect(): lax.psum_scatter(values.astype(jnp.bfloat16), 'mp', scatter_dimension=1,...  130 us
    another operation x1, loops' own time, body(): _, fetched = lax.scan(fetch_one, 0, jnp.arange(UNITS))  118 us
    dot_general x55, matrix products, matmul(): return jnp.einsum(form, left, right, preferred_element_type=single)  107 us
    psum x1, waiting for transfers between devices, body(): lax.psum((jnp.stack([grad_in_proj, grad_out_proj]), loss_local), ('dp', '...  73.2 us
  transfers between devices with their start and end apart: 42, of which 42 were waited for; matrix products, arithmetic and copies ran while one was open for 3% of the time, Pallas kernels for 0%

commit v1 on v0

--- a/solution.py
+++ b/solution.py
@@ -301,7 +301,9 @@
     local_ids = lax.axis_index("dp") * slots + jnp.arange(slots)
     pick = (unit_slot[None, :] == local_ids[:, None]).astype(single)
     live_slot = jnp.sum(pick, axis=1) > 0.5
-    summed = lax.psum(grads, "dp")
+    summed = grads
+    for hop in (1, 2, 4):
+        summed = summed + lax.ppermute(summed, "dp", [(dev, dev ^ hop) for dev in range(8)])
     owned = jnp.einsum("su,ude->sde", pick, summed, precision=highest)
     latent_grad, loss_sum = lax.psum(
         (jnp.stack([grad_in_proj, grad_out_proj]), loss_local), ("dp", "mp")

time: 3450 us -> 4190 us (1.21)
  waiting for transfers between devices: 2770 us -> 3520 us
  local copies, waits for them, and re-layouts: 219 us -> 166 us
    ppermute x0 -> x3, waiting for transfers between devices: none -> 659 us  [body(): lax.ppermute(summed, 'dp', [(dev, dev ^ hop) for dev in range(8)])]
    psum x1, waiting for transfers between devices: 73.2 us -> 727 us  [body(): lax.psum((jnp.stack([grad_in_proj, grad_out_proj]), loss_local), ('dp', '...]
    psum x1 -> x0, waiting for transfers between devices: 571 us -> none  [body(): summed = lax.psum(grads, 'dp')]
    concatenate x1 -> x0, local copies, waits for them, and re-layouts: 46 us -> none  [body(): jnp.concatenate([columns(grad_w_attn, 3), grad_w_self_out[None], grad_w_c...]
  transfers between devices with their start and end apart: 42 -> 44, of which waited for: 42 -> 43; matrix products, arithmetic and copies ran while one was open for 3% -> 1% of each run, Pallas kernels for 0% -> 0%
where the time goes in v1:
time: 4190 us; the launch traced here: 4170 us
  waiting for transfers between devices  3520 us (84%)
  local copies, waits for them, and re-layouts  166 us (4%)
  matrix products  137 us (3%)
  other arithmetic  125 us (3%)
  loops' own time  119 us (3%)
  blocking collectives  78.9 us (2%)
    psum x26, waiting for transfers between devices, broadcast(): return lax.psum(jnp.where(mine, array, jnp.zeros_like(array)), axis)  1830 us
    psum x1, waiting for transfers between devices, body(): lax.psum((jnp.stack([grad_in_proj, grad_out_proj]), loss_local), ('dp', '...  727 us
    ppermute x3, waiting for transfers between devices, body(): lax.ppermute(summed, 'dp', [(dev, dev ^ hop) for dev in range(8)])  659 us
    all_gather x6, waiting for transfers between devices, spread(): return lax.all_gather(values, 'mp', axis=1, tiled=True)  136 us
    reduce_scatter x6, waiting for transfers between devices, collect(): lax.psum_scatter(values.astype(jnp.bfloat16), 'mp', scatter_dimension=1,...  135 us
    another operation x1, loops' own time, body(): _, fetched = lax.scan(fetch_one, 0, jnp.arange(UNITS))  118 us
    dot_general x55, matrix products, matmul(): return jnp.einsum(form, left, right, preferred_element_type=single)  111 us
  transfers between devices with their start and end apart: 44, of which 43 were waited for; matrix products, arithmetic and copies ran while one was open for 1% of the time, Pallas kernels for 0%

profile of v1, /device:TPU:0, one launch (start us, length us, event | category | flops | bytes accessed | tf_op | source)
XLA Modules:
  0.0 4173.2 jit_solution(1273941460478023210)
XLA Ops:
  17.4 2054.3 %while.62 = (s32[]{:T(128)}, bf16[26,192,768]{2,1,0:T(8,128)(2,1)}, s32[26]{0:T(128)S(1)}, s32[26]{0:T(128)S(1)}, s32[26]{0:T(128)S(1)}, /*index=5*/bf16[5,192,7...) while((s32[]{:T(128)}, bf16[26,192,768]{2,1,0:T(8,128)(2,1)}, ...), condition=%wide.region_5.6_spmd, body=%wide.region_3.5_spmd.sunk | while | flops 294924 | bytes 2949439 | solution.py:164
  24.6 73.7 %all-reduce.6.cloned.1.call-done = bf16[1,192,768]{2,1,0:T(8,128)(2,1)} async-done(((bf16[1,192,768]{2,1,0:T(8,128)(2,1)}), bf16[1,192,768]{2,1,0:T(8,128)(2,1)}) %all-reduce.6.cloned.1.call-update) | async-done | bytes 294928 | tf_op jit(solution)/shard_map/while/body/eval_jaxpr/psum | solution.py:28
  107.0 70.1 %all-reduce.6.cloned.1.call-done = bf16[1,192,768]{2,1,0:T(8,128)(2,1)} async-done(((bf16[1,192,768]{2,1,0:T(8,128)(2,1)}), bf16[1,192,768]{2,1,0:T(8,128)(2,1)}) %all-reduce.6.cloned.1.call-update) | async-done | bytes 294928 | tf_op jit(solution)/shard_map/while/body/eval_jaxpr/psum | solution.py:28
  185.9 70.1 %all-reduce.6.cloned.1.call-done = bf16[1,192,768]{2,1,0:T(8,128)(2,1)} async-done(((bf16[1,192,768]{2,1,0:T(8,128)(2,1)}), bf16[1,192,768]{2,1,0:T(8,128)(2,1)}) %all-reduce.6.cloned.1.call-update) | async-done | bytes 294928 | tf_op jit(solution)/shard_map/while/body/eval_jaxpr/psum | solution.py:28
  264.7 70.1 %all-reduce.6.cloned.1.call-done = bf16[1,192,768]{2,1,0:T(8,128)(2,1)} async-done(((bf16[1,192,768]{2,1,0:T(8,128)(2,1)}), bf16[1,192,768]{2,1,0:T(8,128)(2,1)}) %all-reduce.6.cloned.1.call-update) | async-done | bytes 294928 | tf_op jit(solution)/shard_map/while/body/eval_jaxpr/psum | solution.py:28
  343.6 70.1 %all-reduce.6.cloned.1.call-done = bf16[1,192,768]{2,1,0:T(8,128)(2,1)} async-done(((bf16[1,192,768]{2,1,0:T(8,128)(2,1)}), bf16[1,192,768]{2,1,0:T(8,128)(2,1)}) %all-reduce.6.cloned.1.call-update) | async-done | bytes 294928 | tf_op jit(solution)/shard_map/while/body/eval_jaxpr/psum | solution.py:28
  422.5 70.1 %all-reduce.6.cloned.1.call-done = bf16[1,192,768]{2,1,0:T(8,128)(2,1)} async-done(((bf16[1,192,768]{2,1,0:T(8,128)(2,1)}), bf16[1,192,768]{2,1,0:T(8,128)(2,1)}) %all-reduce.6.cloned.1.call-update) | async-done | bytes 294928 | tf_op jit(solution)/shard_map/while/body/eval_jaxpr/psum | solution.py:28
  501.3 70.1 %all-reduce.6.cloned.1.call-done = bf16[1,192,768]{2,1,0:T(8,128)(2,1)} async-done(((bf16[1,192,768]{2,1,0:T(8,128)(2,1)}), bf16[1,192,768]{2,1,0:T(8,128)(2,1)}) %all-reduce.6.cloned.1.call-update) | async-done | bytes 294928 | tf_op jit(solution)/shard_map/while/body/eval_jaxpr/psum | solution.py:28
  580.2 70.1 %all-reduce.6.cloned.1.call-done = bf16[1,192,768]{2,1,0:T(8,128)(2,1)} async-done(((bf16[1,192,768]{2,1,0:T(8,128)(2,1)}), bf16[1,192,768]{2,1,0:T(8,128)(2,1)}) %all-reduce.6.cloned.1.call-update) | async-done | bytes 294928 | tf_op jit(solution)/shard_map/while/body/eval_jaxpr/psum | solution.py:28
  659.1 70.1 %all-reduce.6.cloned.1.call-done = bf16[1,192,768]{2,1,0:T(8,128)(2,1)} async-done(((bf16[1,192,768]{2,1,0:T(8,128)(2,1)}), bf16[1,192,768]{2,1,0:T(8,128)(2,1)}) %all-reduce.6.cloned.1.call-update) | async-done | bytes 294928 | tf_op jit(solution)/shard_map/while/body/eval_jaxpr/psum | solution.py:28
  737.9 70.1 %all-reduce.6.cloned.1.call-done = bf16[1,192,768]{2,1,0:T(8,128)(2,1)} async-done(((bf16[1,192,768]{2,1,0:T(8,128)(2,1)}), bf16[1,192,768]{2,1,0:T(8,128)(2,1)}) %all-reduce.6.cloned.1.call-update) | async-done | bytes 294928 | tf_op jit(solution)/shard_map/while/body/eval_jaxpr/psum | solution.py:28
  816.8 70.1 %all-reduce.6.cloned.1.call-done = bf16[1,192,768]{2,1,0:T(8,128)(2,1)} async-done(((bf16[1,192,768]{2,1,0:T(8,128)(2,1)}), bf16[1,192,768]{2,1,0:T(8,128)(2,1)}) %all-reduce.6.cloned.1.call-update) | async-done | bytes 294928 | tf_op jit(solution)/shard_map/while/body/eval_jaxpr/psum | solution.py:28
  895.7 70.1 %all-reduce.6.cloned.1.call-done = bf16[1,192,768]{2,1,0:T(8,128)(2,1)} async-done(((bf16[1,192,768]{2,1,0:T(8,128)(2,1)}), bf16[1,192,768]{2,1,0:T(8,128)(2,1)}) %all-reduce.6.cloned.1.call-update) | async-done | bytes 294928 | tf_op jit(solution)/shard_map/while/body/eval_jaxpr/psum | solution.py:28
  974.6 70.1 %all-reduce.6.cloned.1.call-done = bf16[1,192,768]{2,1,0:T(8,128)(2,1)} async-done(((bf16[1,192,768]{2,1,0:T(8,128)(2,1)}), bf16[1,192,768]{2,1,0:T(8,128)(2,1)}) %all-reduce.6.cloned.1.call-update) | async-done | bytes 294928 | tf_op jit(solution)/shard_map/while/body/eval_jaxpr/psum | solution.py:28
  1053.5 70.1 %all-reduce.6.cloned.1.call-done = bf16[1,192,768]{2,1,0:T(8,128)(2,1)} async-done(((bf16[1,192,768]{2,1,0:T(8,128)(2,1)}), bf16[1,192,768]{2,1,0:T(8,128)(2,1)}) %all-reduce.6.cloned.1.call-update) | async-done | bytes 294928 | tf_op jit(solution)/shard_map/while/body/eval_jaxpr/psum | solution.py:28
  1132.3 70.1 %all-reduce.6.cloned.1.call-done = bf16[1,192,768]{2,1,0:T(8,128)(2,1)} async-done(((bf16[1,192,768]{2,1,0:T(8,128)(2,1)}), bf16[1,192,768]{2,1,0:T(8,128)(2,1)}) %all-reduce.6.cloned.1.call-update) | async-done | bytes 294928 | tf_op jit(solution)/shard_map/while/body/eval_jaxpr/psum | solution.py:28
  1211.2 70.1 %all-reduce.6.cloned.1.call-done = bf16[1,192,768]{2,1,0:T(8,128)(2,1)} async-done(((bf16[1,192,768]{2,1,0:T(8,128)(2,1)}), bf16[1,192,768]{2,1,0:T(8,128)(2,1)}) %all-reduce.6.cloned.1.call-update) | async-done | bytes 294928 | tf_op jit(solution)/shard_map/while/body/eval_jaxpr/psum | solution.py:28
  1290.1 70.1 %all-reduce.6.cloned.1.call-done = bf16[1,192,768]{2,1,0:T(8,128)(2,1)} async-done(((bf16[1,192,768]{2,1,0:T(8,128)(2,1)}), bf16[1,192,768]{2,1,0:T(8,128)(2,1)}) %all-reduce.6.cloned.1.call-update) | async-done | bytes 294928 | tf_op jit(solution)/shard_map/while/body/eval_jaxpr/psum | solution.py:28
  1368.9 70.1 %all-reduce.6.cloned.1.call-done = bf16[1,192,768]{2,1,0:T(8,128)(2,1)} async-done(((bf16[1,192,768]{2,1,0:T(8,128)(2,1)}), bf16[1,192,768]{2,1,0:T(8,128)(2,1)}) %all-reduce.6.cloned.1.call-update) | async-done | bytes 294928 | tf_op jit(solution)/shard_map/while/body/eval_jaxpr/psum | solution.py:28
  1447.8 70.1 %all-reduce.6.cloned.1.call-done = bf16[1,192,768]{2,1,0:T(8,128)(2,1)} async-done(((bf16[1,192,768]{2,1,0:T(8,128)(2,1)}), bf16[1,192,768]{2,1,0:T(8,128)(2,1)}) %all-reduce.6.cloned.1.call-update) | async-done | bytes 294928 | tf_op jit(solution)/shard_map/while/body/eval_jaxpr/psum | solution.py:28
  1526.7 70.1 %all-reduce.6.cloned.1.call-done = bf16[1,192,768]{2,1,0:T(8,128)(2,1)} async-done(((bf16[1,192,768]{2,1,0:T(8,128)(2,1)}), bf16[1,192,768]{2,1,0:T(8,128)(2,1)}) %all-reduce.6.cloned.1.call-update) | async-done | bytes 294928 | tf_op jit(solution)/shard_map/while/body/eval_jaxpr/psum | solution.py:28
  1605.6 70.1 %all-reduce.6.cloned.1.call-done = bf16[1,192,768]{2,1,0:T(8,128)(2,1)} async-done(((bf16[1,192,768]{2,1,0:T(8,128)(2,1)}), bf16[1,192,768]{2,1,0:T(8,128)(2,1)}) %all-reduce.6.cloned.1.call-update) | async-done | bytes 294928 | tf_op jit(solution)/shard_map/while/body/eval_jaxpr/psum | solution.py:28
  1684.4 70.1 %all-reduce.6.cloned.1.call-done = bf16[1,192,768]{2,1,0:T(8,128)(2,1)} async-done(((bf16[1,192,768]{2,1,0:T(8,128)(2,1)}), bf16[1,192,768]{2,1,0:T(8,128)(2,1)}) %all-reduce.6.cloned.1.call-update) | async-done | bytes 294928 | tf_op jit(solution)/shard_map/while/body/eval_jaxpr/psum | solution.py:28
  1763.3 70.1 %all-reduce.6.cloned.1.call-done = bf16[1,192,768]{2,1,0:T(8,128)(2,1)} async-done(((bf16[1,192,768]{2,1,0:T(8,128)(2,1)}), bf16[1,192,768]{2,1,0:T(8,128)(2,1)}) %all-reduce.6.cloned.1.call-update) | async-done | bytes 294928 | tf_op jit(solution)/shard_map/while/body/eval_jaxpr/psum | solution.py:28
  1842.2 70.1 %all-reduce.6.cloned.1.call-done = bf16[1,192,768]{2,1,0:T(8,128)(2,1)} async-done(((bf16[1,192,768]{2,1,0:T(8,128)(2,1)}), bf16[1,192,768]{2,1,0:T(8,128)(2,1)}) %all-reduce.6.cloned.1.call-update) | async-done | bytes 294928 | tf_op jit(solution)/shard_map/while/body/eval_jaxpr/psum | solution.py:28
  1921.0 70.1 %all-reduce.6.cloned.1.call-done = bf16[1,192,768]{2,1,0:T(8,128)(2,1)} async-done(((bf16[1,192,768]{2,1,0:T(8,128)(2,1)}), bf16[1,192,768]{2,1,0:T(8,128)(2,1)}) %all-reduce.6.cloned.1.call-update) | async-done | bytes 294928 | tf_op jit(solution)/shard_map/while/body/eval_jaxpr/psum | solution.py:28
  1999.9 70.1 %all-reduce.6.cloned.1.call-done = bf16[1,192,768]{2,1,0:T(8,128)(2,1)} async-done(((bf16[1,192,768]{2,1,0:T(8,128)(2,1)}), bf16[1,192,768]{2,1,0:T(8,128)(2,1)}) %all-reduce.6.cloned.1.call-update) | async-done | bytes 294928 | tf_op jit(solution)/shard_map/while/body/eval_jaxpr/psum | solution.py:28
  2101.0 21.8 all-gather.8.cloned.1.call-done
  2141.6 31.6 reduce-scatter.13.cloned.1.call-done
  2177.6 22.3 all-gather.10.cloned.1.call-done
  2215.9 29.8 reduce-scatter.15.cloned.1.call-done
  2252.8 20.8 all-gather.12.cloned.1.call-done
  2285.1 22.3 psum.35
  2325.9 24.0 all-gather.14.cloned.1.call-done
  2362.0 33.0 reduce-scatter.19.cloned.1.call-done
  2402.8 23.5 all-gather.16.cloned.1.call-done
  2430.6 14.6 while.65
  2448.7 33.0 reduce-scatter.21.cloned.1.call-done
  2489.8 23.9 all-gather.18.cloned.1.call-done
  2519.0 29.9 while.66
  2597.2 16.5 reduce-scatter.25.cloned.1.call-done
  2621.6 17.5 reduce-scatter.27.cloned.1.call-done
  2643.8 329.8 %collective-permute-done = f32[26,192,768]{2,1,0:T(8,128)} collective-permute-done((f32[26,192,768]{2,1,0:T(8,128)}, f32[26,192,768]{2,1,0:T(8,128)}, u32[]{:S(2)}, u32[]{:S(2)}) %collective-permute-start) | collective-permute-done | bytes 15335456 | tf_op jit(solution)/shard_map/ppermute | solution.py:306
  2985.8 328.7 %collective-permute-done.1 = f32[26,192,768]{2,1,0:T(8,128)} collective-permute-done((f32[26,192,768]{2,1,0:T(8,128)S(1)}, f32[26,192,768]{2,1,0:T(8,128)}, u32[]{:S(2)}, u32[]{:S(2)}) %collective-permute-start.1) | collective-permute-done | bytes 15335456 | tf_op jit(solution)/shard_map/ppermute | solution.py:306
  3337.3 726.7 %all-reduce.4.cloned.1.call-done = f32[2,20,768]{2,1,0:T(8,128)} async-done(((f32[2,20,768]{2,1,0:T(8,128)}), f32[2,20,768]{2,1,0:T(8,128)}) %all-reduce.4.cloned.1.call-update) | async-done | bytes 122896 | tf_op jit(solution)/shard_map/psum | solution.py:308
  4076.2 15.7 multiply_reduce_fusion.3
  4091.9 42.7 %all-reduce = (f32[]{:T(128)}, f32[]{:T(128)}) all-reduce(f32[]{:T(128)} %get-tuple-element.410, f32[]{:T(128)} %get-tuple-element.412), channel_id=1, replica_groups=mesh['dp'=8,'mp'=4] {'dp','mp'}, use_global_device_ids=true, to_apply=%region_53.54 | all-reduce | flops 2 | bytes 16 | tf_op jit(solution)/shard_map/psum | solution.py:311
  4139.3 15.7 copy_select_fusion
  (691 shorter events, 440.9 us)
Async XLA Ops:
  8.7 2064.2 %copy-start.107 = (f32[2]{0:T(128)}, f32[2]{0:T(128)S(1)}, u32[]{:S(2)}) copy-start(f32[2]{0:T(128)S(1)} %convert_element_type.199) | copy-start | bytes 28
  14.5 2158.6 %copy-start = (f32[2,192,768]{2,1,0:T(8,128)}, f32[2,192,768]{2,1,0:T(8,128)S(1)}, u32[]{:S(2)}) copy-start(f32[2,192,768]{2,1,0:T(8,128)S(1)} %get-tuple-element.408) | copy-start | bytes 3538948
  14.5 2084.0 %copy-start.71 = (f32[2,192]{1,0:T(2,128)}, f32[2,192]{1,0:T(2,128)S(1)}, u32[]{:S(2)}) copy-start(f32[2,192]{1,0:T(2,128)S(1)} %broadcast_multiply_fusion.3) | copy-start | bytes 4612
  14.9 2083.7 %copy-start.81 = (f32[2,192]{1,0:T(2,128)}, f32[2,192]{1,0:T(2,128)S(1)}, u32[]{:S(2)}) copy-start(f32[2,192]{1,0:T(2,128)S(1)} %fusion.191) | copy-start | bytes 4612
  17.4 80.8 %all-reduce.6.cloned.1.call-start = ((), (), s32[]{:S(2)}) async-start(), calls=%async_computation.23 | async-start | bytes 589824 | tf_op jit(solution)/shard_map/while/body/eval_jaxpr/psum | solution.py:28
  100.0 77.2 %all-reduce.6.cloned.1.call-start = ((), (), s32[]{:S(2)}) async-start(), calls=%async_computation.23 | async-start | bytes 589824 | tf_op jit(solution)/shard_map/while/body/eval_jaxpr/psum | solution.py:28
  178.8 77.2 %all-reduce.6.cloned.1.call-start = ((), (), s32[]{:S(2)}) async-start(), calls=%async_computation.23 | async-start | bytes 589824 | tf_op jit(solution)/shard_map/while/body/eval_jaxpr/psum | solution.py:28
  257.7 77.2 %all-reduce.6.cloned.1.call-start = ((), (), s32[]{:S(2)}) async-start(), calls=%async_computation.23 | async-start | bytes 589824 | tf_op jit(solution)/shard_map/while/body/eval_jaxpr/psum | solution.py:28
  336.5 77.2 %all-reduce.6.cloned.1.call-start = ((), (), s32[]{:S(2)}) async-start(), calls=%async_computation.23 | async-start | bytes 589824 | tf_op jit(solution)/shard_map/while/body/eval_jaxpr/psum | solution.py:28
  415.4 77.2 %all-reduce.6.cloned.1.call-start = ((), (), s32[]{:S(2)}) async-start(), calls=%async_computation.23 | async-start | bytes 589824 | tf_op jit(solution)/shard_map/while/body/eval_jaxpr/psum | solution.py:28
  494.3 77.2 %all-reduce.6.cloned.1.call-start = ((), (), s32[]{:S(2)}) async-start(), calls=%async_computation.23 | async-start | bytes 589824 | tf_op jit(solution)/shard_map/while/body/eval_jaxpr/psum | solution.py:28
  573.1 77.2 %all-reduce.6.cloned.1.call-start = ((), (), s32[]{:S(2)}) async-start(), calls=%async_computation.23 | async-start | bytes 589824 | tf_op jit(solution)/shard_map/while/body/eval_jaxpr/psum | solution.py:28
  652.0 77.2 %all-reduce.6.cloned.1.call-start = ((), (), s32[]{:S(2)}) async-start(), calls=%async_computation.23 | async-start | bytes 589824 | tf_op jit(solution)/shard_map/while/body/eval_jaxpr/psum | solution.py:28
  730.9 77.2 %all-reduce.6.cloned.1.call-start = ((), (), s32[]{:S(2)}) async-start(), calls=%async_computation.23 | async-start | bytes 589824 | tf_op jit(solution)/shard_map/while/body/eval_jaxpr/psum | solution.py:28
  809.8 77.2 %all-reduce.6.cloned.1.call-start = ((), (), s32[]{:S(2)}) async-start(), calls=%async_computation.23 | async-start | bytes 589824 | tf_op jit(solution)/shard_map/while/body/eval_jaxpr/psum | solution.py:28
  888.6 77.2 %all-reduce.6.cloned.1.call-start = ((), (), s32[]{:S(2)}) async-start(), calls=%async_computation.23 | async-start | bytes 589824 | tf_op jit(solution)/shard_map/while/body/eval_jaxpr/psum | solution.py:28
  967.5 77.2 %all-reduce.6.cloned.1.call-start = ((), (), s32[]{:S(2)}) async-start(), calls=%async_computation.23 | async-start | bytes 589824 | tf_op jit(solution)/shard_map/while/body/eval_jaxpr/psum | solution.py:28
  1046.4 77.2 %all-reduce.6.cloned.1.call-start = ((), (), s32[]{:S(2)}) async-start(), calls=%async_computation.23 | async-start | bytes 589824 | tf_op jit(solution)/shard_map/while/body/eval_jaxpr/psum | solution.py:28
  1125.3 77.2 %all-reduce.6.cloned.1.call-start = ((), (), s32[]{:S(2)}) async-start(), calls=%async_computation.23 | async-start | bytes 589824 | tf_op jit(solution)/shard_map/while/body/eval_jaxpr/psum | solution.py:28
  1204.1 77.2 %all-reduce.6.cloned.1.call-start = ((), (), s32[]{:S(2)}) async-start(), calls=%async_computation.23 | async-start | bytes 589824 | tf_op jit(solution)/shard_map/while/body/eval_jaxpr/psum | solution.py:28
  1283.0 77.2 %all-reduce.6.cloned.1.call-start = ((), (), s32[]{:S(2)}) async-start(), calls=%async_computation.23 | async-start | bytes 589824 | tf_op jit(solution)/shard_map/while/body/eval_jaxpr/psum | solution.py:28
  1361.9 77.2 %all-reduce.6.cloned.1.call-start = ((), (), s32[]{:S(2)}) async-start(), calls=%async_computation.23 | async-start | bytes 589824 | tf_op jit(solution)/shard_map/while/body/eval_jaxpr/psum | solution.py:28
  1440.7 77.2 %all-reduce.6.cloned.1.call-start = ((), (), s32[]{:S(2)}) async-start(), calls=%async_computation.23 | async-start | bytes 589824 | tf_op jit(solution)/shard_map/while/body/eval_jaxpr/psum | solution.py:28
  1519.6 77.2 %all-reduce.6.cloned.1.call-start = ((), (), s32[]{:S(2)}) async-start(), calls=%async_computation.23 | async-start | bytes 589824 | tf_op jit(solution)/shard_map/while/body/eval_jaxpr/psum | solution.py:28
  1598.5 77.2 %all-reduce.6.cloned.1.call-start = ((), (), s32[]{:S(2)}) async-start(), calls=%async_computation.23 | async-start | bytes 589824 | tf_op jit(solution)/shard_map/while/body/eval_jaxpr/psum | solution.py:28
  1677.4 77.2 %all-reduce.6.cloned.1.call-start = ((), (), s32[]{:S(2)}) async-start(), calls=%async_computation.23 | async-start | bytes 589824 | tf_op jit(solution)/shard_map/while/body/eval_jaxpr/psum | solution.py:28
  1756.2 77.2 %all-reduce.6.cloned.1.call-start = ((), (), s32[]{:S(2)}) async-start(), calls=%async_computation.23 | async-start | bytes 589824 | tf_op jit(solution)/shard_map/while/body/eval_jaxpr/psum | solution.py:28
  1835.1 77.2 %all-reduce.6.cloned.1.call-start = ((), (), s32[]{:S(2)}) async-start(), calls=%async_computation.23 | async-start | bytes 589824 | tf_op jit(solution)/shard_map/while/body/eval_jaxpr/psum | solution.py:28
  1914.0 77.2 %all-reduce.6.cloned.1.call-start = ((), (), s32[]{:S(2)}) async-start(), calls=%async_computation.23 | async-start | bytes 589824 | tf_op jit(solution)/shard_map/while/body/eval_jaxpr/psum | solution.py:28
  1992.9 77.2 %all-reduce.6.cloned.1.call-start = ((), (), s32[]{:S(2)}) async-start(), calls=%async_computation.23 | async-start | bytes 589824 | tf_op jit(solution)/shard_map/while/body/eval_jaxpr/psum | solution.py:28
  2071.7 51.0 %all-gather.8.cloned.1.call-start = ((), (), s32[]{:S(2)}) async-start(), calls=%async_computation.8 | async-start | bytes 2949120 | tf_op jit(solution)/shard_map/all_gather | solution.py:127
  2099.7 73.5 %reduce-scatter.13.cloned.1.call-start = ((), (), s32[]{:S(2)}) async-start(), calls=%async_computation.9 | async-start | bytes 2949120 | tf_op jit(solution)/shard_map/reduce_scatter | solution.py:131
  2140.1 59.8 %all-gather.10.cloned.1.call-start = ((), (), s32[]{:S(2)}) async-start(), calls=%async_computation.10 | async-start | bytes 2949120 | tf_op jit(solution)/shard_map/all_gather | solution.py:127
  2175.8 69.9 %reduce-scatter.15.cloned.1.call-start = ((), (), s32[]{:S(2)}) async-start(), calls=%async_computation.11 | async-start | bytes 2949120 | tf_op jit(solution)/shard_map/reduce_scatter | solution.py:131
  2212.7 60.9 %all-gather.12.cloned.1.call-start = ((), (), s32[]{:S(2)}) async-start(), calls=%async_computation.12 | async-start | bytes 2949120 | tf_op jit(solution)/shard_map/all_gather | solution.py:127
  2249.5 67.1 %reduce-scatter.17.cloned.1.call-start = ((), (), s32[]{:S(2)}) async-start(), calls=%async_computation.13 | async-start | bytes 2949120 | tf_op jit(solution)/shard_map/reduce_scatter | solution.py:131
  2283.6 66.2 %all-gather.14.cloned.1.call-start = ((), (), s32[]{:S(2)}) async-start(), calls=%async_computation.14 | async-start | bytes 2949120 | tf_op jit(solution)/shard_map/all_gather | solution.py:127
  2325.8 69.2 %reduce-scatter.19.cloned.1.call-start = ((), (), s32[]{:S(2)}) async-start(), calls=%async_computation.15 | async-start | bytes 2949120 | tf_op jit(solution)/shard_map/reduce_scatter | solution.py:131
  2361.9 64.4 %all-gather.16.cloned.1.call-start = ((), (), s32[]{:S(2)}) async-start(), calls=%async_computation.16 | async-start | bytes 2949120 | tf_op jit(solution)/shard_map/all_gather | solution.py:127
  2402.3 79.4 %reduce-scatter.21.cloned.1.call-start = ((), (), s32[]{:S(2)}) async-start(), calls=%async_computation.17 | async-start | bytes 2949120 | tf_op jit(solution)/shard_map/reduce_scatter | solution.py:131
  2448.6 65.2 %all-gather.18.cloned.1.call-start = ((), (), s32[]{:S(2)}) async-start(), calls=%async_computation.18 | async-start | bytes 2949120 | tf_op jit(solution)/shard_map/all_gather | solution.py:127
  2489.8 97.1 %reduce-scatter.23.cloned.1.call-start = ((), (), s32[]{:S(2)}) async-start(), calls=%async_computation.19 | async-start | bytes 2949120 | tf_op jit(solution)/shard_map/reduce_scatter | solution.py:131
  2553.8 59.9 %reduce-scatter.25.cloned.1.call-start = ((), (), s32[]{:S(2)}) async-start(), calls=%async_computation.21 | async-start | bytes 245760
  2593.9 45.2 %reduce-scatter.27.cloned.1.call-start = ((), (), s32[]{:S(2)}) async-start(), calls=%async_computation.22 | async-start | bytes 491520
  2618.2 1445.8 %all-reduce.4.cloned.1.call-start = ((), (), s32[]{:S(2)}) async-start(), calls=%async_computation.20 | async-start | bytes 294912 | tf_op jit(solution)/shard_map/psum | solution.py:308
  2642.3 331.3 %collective-permute-start = (f32[26,192,768]{2,1,0:T(8,128)}, f32[26,192,768]{2,1,0:T(8,128)}, u32[]{:S(2)}, u32[]{:S(2)}) collective-permute-start(f32[26,192,768]{2,1,0:T(8,128)} %bitcast.129), channel_id=1, source_target_pairs={{0,4},{4,0},{8,12},{12,8},{16,20},{20,16},{24,28},{28,24},{1,5},{5... | collective-permute-start | bytes 46006280 | tf_op jit(solution)/shard_map/ppermute | solution.py:306
  2984.2 330.2 %collective-permute-start.1 = (f32[26,192,768]{2,1,0:T(8,128)S(1)}, f32[26,192,768]{2,1,0:T(8,128)}, u32[]{:S(2)}, u32[]{:S(2)}) collective-permute-start(f32[26,192,768]{2,1,0:T(8,128)S(1)} %bitcast_add_fusion), channel_id=1, source_target_pairs={{0,8},{4,12},{8,0},{12,4},{16,24},{20,28},{24,16},{28,20},{1,9},{5... | collective-permute-start | bytes 46006280 | tf_op jit(solution)/shard_map/ppermute | solution.py:306
  3326.1 739.5 %collective-permute-start.2 = (f32[26,192,768]{2,1,0:T(8,128)}, f32[26,192,768]{2,1,0:T(8,128)}, u32[]{:S(2)}, u32[]{:S(2)}) collective-permute-start(f32[26,192,768]{2,1,0:T(8,128)} %add.297), channel_id=1, source_target_pairs={{0,16},{4,20},{8,24},{12,28},{16,0},{20,4},{24,8},{28,12},{1,17},{... | collective-permute-start | bytes 46006280 | tf_op jit(solution)/shard_map/ppermute | solution.py:306
  (132 other events, 7983.7 us)
Sparse Core Ops, SparseCore 0:
  24.7 73.5 all-reduce.5
  107.1 69.9 all-reduce.5
  186.0 69.9 all-reduce.5
  264.9 69.9 all-reduce.5
  343.7 69.9 all-reduce.5
  422.6 69.9 all-reduce.5
  501.5 69.9 all-reduce.5
  580.3 69.9 all-reduce.5
  659.2 69.9 all-reduce.5
  738.1 69.9 all-reduce.5
  816.9 69.9 all-reduce.5
  895.8 69.9 all-reduce.5
  974.7 69.9 all-reduce.5
  1053.6 69.9 all-reduce.5
  1132.5 69.9 all-reduce.5
  1211.3 69.9 all-reduce.5
  1290.2 69.9 all-reduce.5
  1369.1 69.9 all-reduce.5
  1447.9 69.9 all-reduce.5
  1526.8 69.9 all-reduce.5
  1605.7 69.9 all-reduce.5
  1684.5 69.9 all-reduce.5
  1763.4 69.9 all-reduce.5
  1842.3 69.9 all-reduce.5
  1921.2 69.9 all-reduce.5
  2000.0 69.9 all-reduce.5
Sparse Core Ops, SparseCore 1:
  2099.8 23.0 all-gather.7
  2140.1 33.0 reduce-scatter.12
  2175.9 23.9 all-gather.9
  2212.7 33.0 reduce-scatter.14
  2249.6 23.9 all-gather.11
  2283.7 32.9 reduce-scatter.16
  2325.9 23.9 all-gather.13
  2362.0 33.0 reduce-scatter.18
  2402.4 23.9 all-gather.15
  2448.7 32.9 reduce-scatter.20
  2489.9 23.9 all-gather.17
  2553.9 33.0 reduce-scatter.22
  2593.9 19.7 reduce-scatter.24
  2618.3 20.7 reduce-scatter.26
  3336.0 727.9 all-reduce.3
